TPU v7x, 32 devices: a whole 2x2x4 slice. The times are simulated.
32 devices in a mesh: grp: 2 (over x), sub: 16 (over z, y, core).
Axes of the slice: x: 2, y: 2, z: 4, core: 2. Of those that a mesh axis runs over, the one named last changes fastest.
Arguments:
- overall_quantity_unnormalized: float32 [16, 16, 256, 128], P(None, 'grp', 'sub'), may hold values from 0.05 to 1
- reservoir_pressure_field: float32 [16, 256, 128], P('grp', 'sub'), may hold values from 0.7 to 1.3
- reservoir_heat_level: float32 [16, 256, 128], P('grp', 'sub'), may hold values from 0.9 to 1.2
- condensed_flag: int32 [16, 256, 128], P('grp', 'sub'), may hold values 0 or 1
- permeability_field: float32 [16, 256, 128], P('grp', 'sub'), may hold values from 0.1 to 10
- pore_capacity: float32 [16, 256, 128], P('grp', 'sub'), may hold values from 0.05 to 0.3
- former_chemical_quantity: float32 [16, 16, 256, 128], P(None, 'grp', 'sub'), may hold values from 0 to 0.03
- transmissibility_multipliers: float32 [3], replicated, may hold values from 0.3 to 3
- viscosity_pair: float32 [2], replicated, may hold values from 0.3 to 3
- crit_kelvin_values: float32 [16], replicated, may hold values from 0.3 to 2.5
- attraction_parameters: float32 [16], replicated, may hold values from 0.3 to 4
- repulsive_parameters: float32 [16], replicated, may hold values from 0.02 to 0.15
- attraction_thermal_gradients: float32 [16], replicated, may hold values from 0.3 to 1.2
- binary_coupling_matrix: float32 [16, 16], replicated, may hold values from 0 to 0.3, as said below
- injected_recipe_unnormalized: float32 [16], replicated, may hold values from 0.05 to 1
- perforated_locale: int32 [8192], P(('grp', 'sub')), may hold values from 0 to 16383
- perforated_member: int32 [8192, 1], P(('grp', 'sub')), may hold values from 0 to 15; in each aligned block of 256 rows (0 to 255, 256 to 511, ...) at most 40 rows name the same one
- connection_conduit_piece: int32 [8192], P(('grp', 'sub')), may hold values from 0 to 31
- connection_inflow_strength: float32 [8192], P(('grp', 'sub')), may hold values from 0.02 to 0.2
- group_member_place: int32 [2, 16], P('grp'), may hold values from 0 to 15, each once within a row
- conduit_pieces_toe_forward: int32 [32, 32], P(('grp', 'sub')), may hold values from 0 to 31, each once within a row
- conduit_piece_pressures: float32 [32, 32], P(('grp', 'sub')), may hold values from 0.7 to 1.3
- downstream_exit_pressure: float32 [32], P(('grp', 'sub')), may hold values from 0.6 to 1.2
- friction_factors: float32 [32], P(('grp', 'sub')), may hold values from 3.0517578e-05 to 0.00030517578
Outputs:
- residual: float32 [16, 16, 256, 128], P(None, 'grp', 'sub')
- ln_phi: bfloat16 [16, 16, 256, 128], P(None, 'grp', 'sub')
- well_residual: float32 [32, 32], P(('grp', 'sub'))
Inputs may be any that keep to these rules, and one draw needn't show every extreme that they name: `perforated_locale`: flattened index (first, second, layer) of a cell of the listing device's own block. `perforated_member`: a well of the listing device's group; among the 256 rows of one device at most 40 name the same well. `group_member_place`: each row is a permutation; slot j of a group lies on the group's device j. `conduit_pieces_toe_forward`: each row is a permutation of the segments. `binary_coupling_matrix`: symmetric with zero diagonal.
All inputs are finite; a program needn't handle non-finite values. No bound on the sum of `condensed_flag` on one device may be relied on, other than what follows from the above.
Results may differ from a plain program's by a relative error of at most 0.001.
Values sent between devices are 32-bit elements; how exact they have to be, the bound alone decides.
No kernel may reach another device: no remote copies, remote signals or barrier semaphores. Data moves between devices by JAX's collectives and lax.ppermute only.
A program may use at most 64 MiB of HBM per device.

v0:
```python
import functools
import math

import jax
import jax.numpy as jnp
from jax import lax
from jax.experimental import pallas as pl
from jax.experimental.pallas import tpu as pltpu
from jax.sharding import PartitionSpec as P

NEWT = 8
ROOT_TWO = math.sqrt(2.0)
LANES = 128
SUBLANES = 8
F32 = jnp.float32
BF16 = jnp.bfloat16
VMEM_LIMIT = 48 * 1024 * 1024
MARGIN = 8
WHOLE = (
    "coupling", "crit", "attract", "slope", "covol", "heat", "press", "loc", "member", "place",
    "flag", "visc", "trans", "inject", "seg", "strength", "own_press", "perm",
)


def iota(shape, dim):
    return lax.broadcasted_iota(jnp.int32, shape, dim)


def pieces_of(x, count):
    out = []
    for _ in range(count):
        piece = x.astype(BF16)
        out.append(piece)
        x = x - piece.astype(F32)
    return out


def mat(a, b):
    return lax.dot_general(a, b, (((1,), (0,)), ((), ())), preferred_element_type=F32)


def mat_nt(a, b):
    return lax.dot_general(a, b, (((1,), (1,)), ((), ())), preferred_element_type=F32)


def mat_hot(x, hot, count=3):
    return sum(mat(piece, hot) for piece in pieces_of(x, count))


def hot_mat_nt(hot, x, count=3):
    return sum(mat_nt(hot, piece) for piece in pieces_of(x, count))


def inverse(x):
    r = pl.reciprocal(x, approx=True)
    return r * (2.0 - x * r)


def hot(cond):
    return jnp.where(cond, 1.0, 0.0).astype(BF16)


def place_hots(loc, rows):
    n = loc.shape[1]
    row_hot = iota((rows, n), 0) == loc // LANES
    lane_hot = iota((LANES, n), 0) == loc % LANES
    return row_hot, lane_hot


def slot_hot_of(member, place):
    wells = place.shape[1]
    slot_of = hot(iota((wells, wells), 0) == wells - 1 - place)
    member_hot = hot(iota((wells, member.shape[1]), 0) == member)
    return mat(slot_of, member_hot)


def phase_kernel(
    nx,
    ny,
    axes,
    amount,
    *rest,
):
    sources, rest = rest[: len(WHOLE)], rest[len(WHOLE) :]
    (
        psi_v,
        terms_out,
        carried_out,
        mob_out,
        edge_x_out,
        edge_ya_out,
        edge_yb_out,
        part_out,
        pcell_out,
        consts_out,
    ) = rest[:10]
    targets, rest = rest[10 : 10 + len(WHOLE)], rest[10 + len(WHOLE) :]
    amount_v, split_v, field_v, table_v, small_sems, in_sems = rest
    nc = amount.shape[0]
    per = 2
    chunks = nx // per
    half = chunks // 2
    rows = per * ny

    def go(source, target, sem):
        copy = pltpu.make_async_copy(source, target, sem)
        copy.start()
        return copy

    loads, copies = [], {}
    for k, name in enumerate(WHOLE):
        if name in ("press", "flag"):
            span = pl.ds(len(loads) * half * rows, half * rows)
            loads.append(go(amount.at[:, span], amount_v.at[:, span], in_sems.at[len(loads)]))
        copies[name] = go(sources[k], targets[k], small_sems.at[k])

    def arrived(*names):
        for name in names:
            copies[name].wait()
        return [targets[WHOLE.index(name)] for name in names]

    size = nc * ny
    spread = hot(iota((size, nc), 0) // ny == iota((size, nc), 1))
    same_row = iota((size, size), 0) % ny == iota((size, size), 1) % ny
    mixers = []
    (coupling,) = arrived("coupling")
    for piece in pieces_of(1.0 - coupling[...], 2):
        wide = mat(spread, piece).astype(BF16)
        mixers.append(jnp.where(same_row, mat_nt(wide, spread), 0.0).astype(BF16))
    mixer = jnp.concatenate([mixers[0], mixers[0], mixers[1]], axis=1)

    crit, attract, slope, covol = arrived("crit", "attract", "slope", "covol")
    for i in range(nc):
        root = jnp.sqrt(jnp.full((SUBLANES, LANES), attract[i], F32))
        kappa = jnp.full((SUBLANES, LANES), slope[i], F32)
        tc = jnp.full((SUBLANES, LANES), crit[i], F32)
        table_v[0, i] = root * (1.0 + kappa)
        table_v[1, i] = root * kappa / jnp.sqrt(tc)
        table_v[2, i] = jnp.full((SUBLANES, LANES), covol[i], F32)

    press, loc, member, place = arrived("press", "loc", "member", "place")
    row_hot, lane_hot = place_hots(loc[...], nx * ny)
    lane_hot = hot(lane_hot)

    def cells_of(field, count):
        found = mat_hot(field, lane_hot, count)
        return jnp.sum(jnp.where(row_hot, found, 0.0), axis=0, keepdims=True)

    p_cell = cells_of(press[...], 3)
    pcell_out[...] = p_cell
    slot_hot = slot_hot_of(member[...], place[...]).astype(BF16)
    (heat,) = arrived("heat")

    shape3 = (ny // SUBLANES, SUBLANES, LANES)
    for h in range(2):
        loads[h].wait()
        for c in range(h * half, (h + 1) * half):
            for x in range(c * per, (c + 1) * per):
                span = pl.ds(x * ny, ny)
                lanes = pl.ds(x * LANES, LANES)
                root_t = jnp.sqrt(heat[span].reshape(shape3))
                total = jnp.zeros(shape3, F32)
                volume = jnp.zeros(shape3, F32)
                for i in range(nc):
                    o = amount_v[i, span].reshape(shape3)
                    v = jnp.abs(table_v[0, i] - table_v[1, i] * root_t) * o
                    total += o
                    volume += table_v[2, i] * o
                    high, low = pieces_of(v.reshape(ny, LANES), 2)
                    split_v[pl.ds(i * ny, ny), lanes] = high
                    split_v[pl.ds(size + i * ny, ny), lanes] = low
                    split_v[pl.ds(2 * size + i * ny, ny), lanes] = high
                field_v[0, span] = total.reshape(ny, LANES)
                field_v[1, span] = volume.reshape(ny, LANES)
            lanes = pl.ds(c * per * LANES, per * LANES)
            mixed = mat(mixer, split_v[:, lanes])
            for k in range(per):
                x = c * per + k
                span = pl.ds(x * ny, ny)
                root_t = jnp.sqrt(heat[span].reshape(shape3))
                total = jnp.zeros(shape3, F32)
                for i in range(nc):
                    m = mixed[i * ny : (i + 1) * ny, k * LANES : (k + 1) * LANES].reshape(shape3)
                    psi = jnp.abs(table_v[0, i] - table_v[1, i] * root_t) * m
                    total += amount_v[i, span].reshape(shape3) * psi
                    psi_v[i, span] = psi.reshape(ny, LANES)
                field_v[2, span] = total.reshape(ny, LANES)

        if h == 0:
            flag, visc, trans, inject = arrived("flag", "visc", "trans", "inject")
        span = pl.ds(h * half * rows, half * rows)
        p, t = press[span], heat[span]
        liquid = flag[span] == 1
        r = inverse(field_v[0, span])
        rt = inverse(t)
        ratio_pt = p * rt
        g = ratio_pt * rt
        beta = field_v[1, span] * r
        gr = g * r
        big_a = gr * r * field_v[2, span]
        big_b = ratio_pt * beta
        z = jnp.where(liquid, big_b + 0.01, 1.0 + big_b)
        floor = big_b + 0.01
        c2 = big_b - 1.0
        c1 = big_a - 3.0 * big_b * big_b - 2.0 * big_b
        c0 = big_b * big_b + big_b * big_b * big_b - big_a * big_b
        twice = 2.0 * c2
        for _ in range(NEWT):
            value = ((z + c2) * z + c1) * z + c0
            incline = (3.0 * z + twice) * z + c1
            z = jnp.maximum(z - value * inverse(jnp.maximum(incline, 0.1)), floor)
        log_ratio = jnp.log(
            (z + (1.0 + ROOT_TWO) * big_b) * inverse(z + (1.0 - ROOT_TWO) * big_b)
        )
        lb = log_ratio * inverse(ROOT_TWO * big_b)
        e0 = jnp.log(z - big_b)
        e1 = (z - 1.0 + 0.5 * big_a * lb) * inverse(beta)
        e2 = gr * lb
        mob = ratio_pt * inverse(z * jnp.where(liquid, visc[1], visc[0]))
        mob_out[span] = mob
        terms_out[0, span] = e0
        terms_out[1, span] = e1
        terms_out[2, span] = e2
        field_v[3, span] = mob * r
        for x in range(h * half * per, (h + 1) * half * per):
            span = pl.ds(x * ny, ny)
            mr = field_v[3, span]
            for i in range(nc):
                carried_out[i, pl.ds(MARGIN + x * ny, ny)] = mr * amount_v[i, span]

    total = sum(inject[i] for i in range(nc))
    share = 1.0 / jnp.full((SUBLANES, LANES), total, F32)
    numbers = [trans[0], trans[1], trans[2], visc[0], visc[1]]
    for i in range(nc):
        consts_out[i] = inject[i] * share
        consts_out[nc + 8 + i] = table_v[2, i]
    for i, number in enumerate(numbers):
        consts_out[nc + i] = jnp.full((SUBLANES, LANES), number, F32)

    seg, strength, own_press, perm = arrived("seg", "strength", "own_press", "perm")
    weight = strength[...] * cells_of(mob_out[...], 2)
    segments = own_press.shape[1]
    place_of = iota((LANES, loc.shape[1]), 0)
    sums = jnp.where(place_of == seg[...], weight, 0.0)
    sums += jnp.where(place_of == seg[...] + segments, weight * (p_cell - 1.0), 0.0)
    shift = hot(iota((segments, LANES), 0) + 2 * segments == iota((segments, LANES), 1))
    part_out[...] = hot_mat_nt(slot_hot, sums, 2) + mat_hot(own_press[...], shift)

    odd_g = lax.axis_index(axes[0]) % 2 == 1
    odd_s = lax.axis_index(axes[1]) % 2 == 1
    for k in range(edge_x_out.shape[0]):
        at_low = odd_g if k == 0 else jnp.logical_not(odd_g)
        start = pl.multiple_of(jnp.where(at_low, 0, (nx - 1) * ny), ny)
        for i in range(nc):
            edge_x_out[k, i] = carried_out[i, pl.ds(start + MARGIN, ny)]
        edge_x_out[k, nc] = press[pl.ds(start, ny)]
        edge_x_out[k, nc + 1] = perm[pl.ds(start, ny)]
    for i in range(nc + 2):
        source = carried_out.at[i] if i < nc else press if i == nc else perm
        skip = MARGIN if i < nc else 0
        low = source[pl.ds(skip, nx, stride=ny)]
        high = source[pl.ds(skip + ny - 1, nx, stride=ny)]
        edge_ya_out[i] = jnp.where(odd_s, low, high)
        edge_yb_out[i] = jnp.where(odd_s, high, low)


def fugacity_kernel(ny, psi, terms, consts, lnphi_out, lnphi_v, sems):
    nc, rows, _ = psi.shape
    shape3 = (ny // SUBLANES, SUBLANES, LANES)
    parts = sems.shape[0]
    stores = []
    for part in range(parts):
        for x in range(part * rows // parts // ny, (part + 1) * rows // parts // ny):
            span = pl.ds(x * ny, ny)
            e0, e1, e2 = (terms[k, span].reshape(shape3) for k in range(3))
            for i in range(nc):
                value = consts[nc + 8 + i] * e1 - e0 - psi[i, span].reshape(shape3) * e2
                lnphi_v[i, span] = value.reshape(ny, LANES).astype(BF16)
        span = pl.ds(part * rows // parts, rows // parts)
        copy = pltpu.make_async_copy(lnphi_v.at[:, span], lnphi_out.at[:, span], sems.at[part])
        copy.start()
        stores.append(copy)
    for copy in stores:
        copy.wait()


def flux_kernel(
    nx,
    ny,
    axes,
    many_x,
    carried,
    press,
    perm,
    pore,
    flag,
    mob,
    old,
    edge_ya,
    edge_yb,
    well_rows,
    loc,
    member,
    seg,
    strength,
    place,
    pcell,
    consts,
    own_press,
    order,
    exit_press,
    friction,
    *rest,
):
    edge_x, (resid_out, well_out, y_v, res_v, out_sems) = rest[:many_x], rest[many_x:]
    nc = carried.shape[0]
    g, s = lax.axis_index(axes[0]), lax.axis_index(axes[1])
    ng, ns = lax.axis_size(axes[0]), lax.axis_size(axes[1])
    odd_g, odd_s = g % 2 == 1, s % 2 == 1
    has_low_y, has_high_y = s > 0, s < ns - 1
    has_low_x, has_high_x = g > 0, g < ng - 1

    for i in range(nc + 2):
        a, b = edge_ya[i], edge_yb[i]
        low, high = jnp.where(odd_s, a, b), jnp.where(odd_s, b, a)
        if i == nc + 1:
            low, high = jnp.where(has_low_y, low, 0.0), jnp.where(has_high_y, high, 0.0)
        y_v[0, i] = low
        y_v[1, i] = high

    def side_x(i, high):
        if many_x == 1:
            return edge_x[0][i]
        return jnp.where(odd_g != high, edge_x[0][i], edge_x[1][i])

    row_hot, lane_hot = place_hots(loc[...], nx * ny)
    slot_hot = slot_hot_of(member[...], place[...])
    segments = own_press.shape[1]
    gathered = well_rows[...]
    seg_hot = hot(iota((LANES, loc.shape[1]), 0) == seg[...] + 2 * segments)
    p_seg = jnp.sum(mat_hot(gathered, seg_hot) * slot_hot, axis=0, keepdims=True)
    push = strength[...] * (pcell[...] - p_seg)
    flows = jnp.concatenate(
        [
            jnp.where(lane_hot, jnp.maximum(push, 0.0), 0.0),
            jnp.where(lane_hot, jnp.minimum(push, 0.0), 0.0),
        ],
        axis=0,
    )
    spread = hot_mat_nt(hot(row_hot), flows, 2)

    own = jnp.sum(gathered, axis=0, keepdims=True)
    well_p = own_press[...]
    rate = own[:, segments : 2 * segments] - (well_p - 1.0) * own[:, :segments]
    order_hot = hot(iota((segments, segments), 0) == order[...])
    both = mat_hot(jnp.concatenate([rate, well_p], axis=0), order_hot)
    upper = hot(iota((segments, segments), 0) <= iota((segments, segments), 1))
    running = mat_hot(both[0:1], upper)
    press_ord = both[1:2]
    after = hot(iota((segments, segments), 0) == iota((segments, segments), 1) + 1)
    last = iota((1, segments), 1) == segments - 1
    nexts = jnp.where(last, exit_press[...], mat_hot(press_ord, after))
    res_ord = press_ord - nexts - friction[...] * running * jnp.abs(running)
    well_out[...] = sum(mat_nt(piece, order_hot) for piece in pieces_of(res_ord, 3))

    lane = iota((ny, LANES), 1)
    row = iota((ny, LANES), 0)
    first, final = row == 0, row == ny - 1

    def const(k):
        return jnp.concatenate([consts[k]] * (ny // SUBLANES), axis=0)

    stores = []
    for x in range(nx):
        rows = pl.ds(x * ny, ny)
        p_a, k_a = press[rows], perm[rows]
        twice_k = 2.0 * k_a

        def face(p_b, k_b, axis):
            t = const(nc + axis) * (twice_k * k_b) * inverse(k_a + k_b)
            flow = t * (p_a - p_b)
            return jnp.maximum(flow, 0.0), jnp.minimum(flow, 0.0)

        def other_x(field, i, high):
            at = x + 1 if high else x - 1
            return field[pl.ds(at * ny, ny)] if 0 <= at < nx else side_x(i, high)

        def other_y(field, i, high):
            if high:
                return jnp.where(final, y_v[1, i, pl.ds(x, 1)], pltpu.roll(field, ny - 1, 0))
            return jnp.where(first, y_v[0, i, pl.ds(x, 1)], pltpu.roll(field, 1, 0))

        centre = pore[rows] * jnp.where(flag[rows] == 1, const(nc + 4), const(nc + 3))
        centre += spread[x * ny : (x + 1) * ny, :LANES]
        ins = []
        for high in (True, False):
            p_b, k_b = other_x(press, nc, high), other_x(perm, nc + 1, high)
            if x == nx - 1 and high:
                k_b = jnp.where(has_high_x, k_b, 0.0)
            if x == 0 and not high:
                k_b = jnp.where(has_low_x, k_b, 0.0)
            ins.append(face(p_b, k_b, 0))
        for high in (True, False):
            ins.append(face(other_y(p_a, nc, high), other_y(k_a, nc + 1, high), 1))
        for shift, edge in ((LANES - 1, LANES - 1), (1, 0)):
            k_b = jnp.where(lane == edge, 0.0, pltpu.roll(k_a, shift, 1))
            ins.append(face(pltpu.roll(p_a, shift, 1), k_b, 2))
        for out, _ in ins:
            centre += out
        ins = [into for _, into in ins]
        pushed = mob[rows] * spread[x * ny : (x + 1) * ny, LANES:]
        for i in range(nc):
            base = MARGIN + x * ny
            c = carried[i, pl.ds(base, ny)]
            value = centre * c - old[i, rows] + const(i) * pushed
            for k, high in ((0, True), (1, False)):
                at = x + 1 if high else x - 1
                inside = 0 <= at < nx
                c_b = carried[i, pl.ds(MARGIN + at * ny, ny)] if inside else side_x(i, high)
                value += ins[k] * c_b
            up, down = carried[i, pl.ds(base + 1, ny)], carried[i, pl.ds(base - 1, ny)]
            value += ins[2] * jnp.where(final, y_v[1, i, pl.ds(x, 1)], up)
            value += ins[3] * jnp.where(first, y_v[0, i, pl.ds(x, 1)], down)
            value += ins[4] * pltpu.roll(c, LANES - 1, 1)
            value += ins[5] * pltpu.roll(c, 1, 1)
            res_v[i, rows] = value
        copy = pltpu.make_async_copy(res_v.at[:, rows], resid_out.at[:, rows], out_sems.at[x])
        copy.start()
        stores.append(copy)
    for copy in stores:
        copy.wait()


def swaps_of(count, other):
    pairs = [(i, i + 1) for i in range(1 if other else 0, count - 1, 2)]
    return pairs + [(b, a) for a, b in pairs]


def other_swaps_of(groups, count):
    swaps = [(g * count + a, g * count + b) for g in range(groups) for a, b in swaps_of(count, True)]
    ends = [(g * count + e, (g ^ 1) * count + e) for g in range(groups) for e in (0, count - 1)]
    return sorted(swaps + ends)


def per_device(
    amount,
    press,
    heat,
    flag,
    perm,
    pore,
    old,
    trans,
    visc,
    crit,
    attract,
    covol,
    slope,
    coupling,
    inject,
    locale,
    member,
    seg,
    strength,
    place,
    order,
    seg_press,
    exit_press,
    friction,
):
    axes = ("grp", "sub")
    nc, nx, ny, nz = amount.shape
    ng, ns = lax.axis_size("grp"), lax.axis_size("sub")
    rows = nx * ny
    perfs = locale.shape[0]
    wells, segments = place.shape[1], seg_press.shape[1]
    flat = lambda a: a.reshape(a.shape[:-3] + (rows, nz))
    line = lambda a: a.reshape(1, perfs)
    vm = pl.BlockSpec(memory_space=pltpu.VMEM)
    hbm = pl.BlockSpec(memory_space=pltpu.HBM)
    many_x = 1 if ng == 2 else 2

    amount, old = flat(amount), flat(old)
    press, heat, flag, perm, pore = (flat(a) for a in (press, heat, flag, perm, pore))
    locale, member, seg, strength = (line(a) for a in (locale, member, seg, strength))
    exit_press, friction = exit_press.reshape(1, 1), friction.reshape(1, 1)

    sources = (
        coupling, crit, attract, slope, covol, heat, press, locale, member, place,
        flag, visc, trans, inject, seg, strength, seg_press, perm,
    )
    kept = [
        pltpu.SMEM(a.shape, a.dtype) if a.ndim == 1 else pltpu.VMEM(a.shape, a.dtype)
        for a in sources
    ]
    in_hbm = lambda a: pltpu.with_memory_space_constraint(a, pltpu.HBM)

    psi, terms, carried, mob, edge_x, edge_ya, edge_yb, part, pcell, consts = pl.pallas_call(
        functools.partial(phase_kernel, nx, ny, axes),
        out_shape=(
            jax.ShapeDtypeStruct((nc, rows, nz), F32),
            jax.ShapeDtypeStruct((3, rows, nz), F32),
            jax.ShapeDtypeStruct((nc, rows + 2 * MARGIN, nz), F32),
            jax.ShapeDtypeStruct((rows, nz), F32),
            jax.ShapeDtypeStruct((many_x, nc + 2, ny, nz), F32),
            jax.ShapeDtypeStruct((nc + 2, nx, nz), F32),
            jax.ShapeDtypeStruct((nc + 2, nx, nz), F32),
            jax.ShapeDtypeStruct((wells, LANES), F32),
            jax.ShapeDtypeStruct((1, perfs), F32),
            jax.ShapeDtypeStruct((2 * nc + 8, SUBLANES, LANES), F32),
        ),
        in_specs=[hbm] * (1 + len(sources)),
        out_specs=(vm,) * 10,
        scratch_shapes=[
            *kept,
            pltpu.VMEM((nc, rows, nz), F32),
            pltpu.VMEM((3 * nc * ny, nx * nz), BF16),
            pltpu.VMEM((4, rows, nz), F32),
            pltpu.VMEM((3, nc, SUBLANES, LANES), F32),
            pltpu.SemaphoreType.DMA((len(sources),)),
            pltpu.SemaphoreType.DMA((2,)),
        ],
        compiler_params=pltpu.CompilerParams(vmem_limit_bytes=VMEM_LIMIT),
        name="phase",
    )(in_hbm(amount), *(in_hbm(a) for a in sources))

    backward = [list(range(ns))[::-1]]
    well_rows = lax.all_to_all(
        part, "sub", split_axis=0, concat_axis=0, axis_index_groups=backward, tiled=True
    )
    got_x = [lax.ppermute(edge_x[k], "grp", swaps_of(ng, k == 1)) for k in range(many_x)]
    got_yb = lax.ppermute(edge_yb, axes, other_swaps_of(ng, ns))
    got_ya = lax.ppermute(edge_ya, "sub", swaps_of(ns, False))

    lnphi = pl.pallas_call(
        functools.partial(fugacity_kernel, ny),
        out_shape=jax.ShapeDtypeStruct((nc, rows, nz), BF16),
        in_specs=[vm] * 3,
        out_specs=hbm,
        scratch_shapes=[pltpu.VMEM((nc, rows, nz), BF16), pltpu.SemaphoreType.DMA((4,))],
        compiler_params=pltpu.CompilerParams(vmem_limit_bytes=VMEM_LIMIT),
        cost_estimate=pl.CostEstimate(
            flops=8 * nc * rows * nz, bytes_accessed=32 * nc * rows * nz, transcendentals=0
        ),
        name="fugacity",
    )(psi, terms, consts)

    resid, well = pl.pallas_call(
        functools.partial(flux_kernel, nx, ny, axes, many_x),
        out_shape=(
            jax.ShapeDtypeStruct((nc, rows, nz), F32),
            jax.ShapeDtypeStruct((1, segments), F32),
        ),
        in_specs=[vm] * (21 + many_x),
        out_specs=(hbm, vm),
        scratch_shapes=[
            pltpu.VMEM((2, nc + 2, nx, nz), F32),
            pltpu.VMEM((nc, rows, nz), F32),
            pltpu.SemaphoreType.DMA((nx,)),
        ],
        compiler_params=pltpu.CompilerParams(vmem_limit_bytes=VMEM_LIMIT),
        name="flux",
    )(
        carried, press, perm, pore, flag, mob, old, got_ya, got_yb, well_rows,
        locale, member, seg, strength, place, pcell,
        consts, seg_press, order, exit_press, friction, *got_x,
    )
    block = (nc, nx, ny, nz)
    return resid.reshape(block), lnphi.reshape(block), well


def solution(mesh):
    cells, parts = P("grp", "sub", None), P(None, "grp", "sub", None)
    listed = P(("grp", "sub"))
    row = P(("grp", "sub"), None)
    in_specs = (
        (parts,) + (cells,) * 5 + (parts,) + (P(),) * 8
        + (listed, row, listed, listed, P("grp", None), row, row, listed, listed)
    )
    return jax.shard_map(
        per_device, mesh=mesh, in_specs=in_specs, out_specs=(parts, parts, row), check_vma=False
    )
```

profile of v0, /device:TPU:0, one launch (start us, length us, event | category | flops | bytes accessed | tf_op | source)
XLA Modules:
  0.0 27.9 jit_solution(14990994908531150939)
XLA Ops:
  0.6 0.0 copy-start.9
  0.6 0.0 copy-start.10
  0.7 0.0 copy-start.11
  0.7 0.0 copy-start.12
  0.7 0.0 copy-start.13
  0.7 0.0 copy-start.14
  0.7 0.0 copy-start.15
  0.7 4.5 %phase.1 = (f32[16,128,128]{2,1,0:T(8,128)S(1)}, f32[3,128,128]{2,1,0:T(8,128)S(1)}, f32[16,144,128]{2,1,0:T(8,128)S(1)}, f32[128,128]{1,0:T(8,128)S(1)}, f32[1,...) custom-call(f32[16,128,128]{2,1,0:T(8,128)} %bitcast.39, ...), custom_call_target="tpu_custom_call" | custom-call | tf_op jit(solution)/shard_map/phase/pallas_call | solution.py:498
  5.2 0.0 copy-start.4
  5.2 0.7 %copy-done.4 = f32[3,128,128]{2,1,0:T(8,128)} copy-done((f32[3,128,128]{2,1,0:T(8,128)}, f32[3,128,128]{2,1,0:T(8,128)S(1)}, u32[]{:S(2)}) %copy-start.4) | copy-done | bytes 196632
  5.9 0.0 copy-start.7
  5.9 0.6 %copy-done.7 = f32[128,128]{1,0:T(8,128)} copy-done((f32[128,128]{1,0:T(8,128)}, f32[128,128]{1,0:T(8,128)S(1)}, u32[]{:S(2)}) %copy-start.7) | copy-done | bytes 65560
  6.5 0.0 copy-start
  6.5 0.0 copy-start.1
  6.5 2.9 %collective-permute-start.2 = (f32[18,16,128]{2,1,0:T(8,128)}, f32[18,16,128]{2,1,0:T(8,128)}, u32[]{:S(2)}, u32[]{:S(2)}) collective-permute-start(f32[18,16,128]{2,1,0:T(8,128)} %bitcast.16), channel_id=1, source_target_pairs={{0,16},{16,0},{1,17},{17,1},{2,18},{18,2},{3,19},{19,3},{4,20},{20... | collective-permute-start | bytes 442376 | tf_op jit(solution)/shard_map/ppermute | solution.py:531
  9.5 0.0 collective-permute-start
  9.5 0.1 collective-permute-start.1
  9.5 8.2 %all-to-all-start = ((f32[16,1,128]{2,1,0:T(1,128)}), f32[16,1,128]{2,1,0:T(1,128)S(1)}, u32[]{:S(2)}, u32[]{:S(2)}) async-start(f32[16,1,128]{2,1,0:T(1,128)} %bitcast.12), calls=%async_computation | async-start | bytes 16384 | tf_op jit(solution)/shard_map/all_to_all | solution.py:528
  19.0 0.0 copy-start.5
  19.1 0.9 %copy-done.5 = f32[3,128,128]{2,1,0:T(8,128)S(1)} copy-done((f32[3,128,128]{2,1,0:T(8,128)S(1)}, f32[3,128,128]{2,1,0:T(8,128)}, u32[]{:S(2)}) %copy-start.5) | copy-done | bytes 196632
  20.0 0.9 %fugacity.1 = bf16[16,128,128]{2,1,0:T(8,128)(2,1)} custom-call(f32[16,128,128]{2,1,0:T(8,128)S(1)} %get-tuple-element.24.psi, f32[3,128,128]{2,1,0:T(8,128)S(1)} %copy-done.5, f32[40,8,128]{2,1,0:T(8,128)S(1)} %get-tuple-element.21.consts), custom_call_target="tpu_custom_call" | custom-call | flops 2097152 | bytes 8388608 | tf_op jit(solution)/shard_map/fugacity/pallas_call | solution.py:535
  20.8 0.0 all-to-all-done
  20.8 0.0 collective-permute-done.edge_ya
  20.9 0.0 collective-permute-done.1.edge_yb
  20.9 0.0 collective-permute-done.2.rest_0_
  20.9 0.0 copy-done.9
  20.9 0.0 copy-done.10
  20.9 0.0 copy-done.11
  20.9 0.0 copy-done.12
  20.9 0.0 copy-done.13
  20.9 0.0 copy-done.14
  20.9 0.0 copy-done.15
  20.9 0.0 copy-done
  21.0 0.0 copy-done.1
  21.0 0.0 copy-start.2
  21.0 0.8 %copy-done.2 = s32[8,16,128]{2,1,0:T(8,128)S(1)} copy-done((s32[8,16,128]{2,1,0:T(8,128)S(1)}, s32[8,16,128]{2,1,0:T(8,128)}, u32[]{:S(2)}) %copy-start.2) | copy-done | bytes 65560
  21.8 0.0 copy-start.3
  21.8 0.8 %copy-done.3 = f32[8,16,128]{2,1,0:T(8,128)S(1)} copy-done((f32[8,16,128]{2,1,0:T(8,128)S(1)}, f32[8,16,128]{2,1,0:T(8,128)}, u32[]{:S(2)}) %copy-start.3) | copy-done | bytes 65560
  22.7 0.0 copy-start.6
  22.7 0.8 %copy-done.6 = f32[8,16,128]{2,1,0:T(8,128)S(1)} copy-done((f32[8,16,128]{2,1,0:T(8,128)S(1)}, f32[8,16,128]{2,1,0:T(8,128)}, u32[]{:S(2)}) %copy-start.6) | copy-done | bytes 65560
  23.5 0.0 copy-start.8
  23.5 0.8 %copy-done.8 = f32[128,128]{1,0:T(8,128)S(1)} copy-done((f32[128,128]{1,0:T(8,128)S(1)}, f32[128,128]{1,0:T(8,128)}, u32[]{:S(2)}) %copy-start.8) | copy-done | bytes 65560
  24.3 3.5 %flux.1 = (f32[16,128,128]{2,1,0:T(8,128)}, f32[1,32]{1,0:T(1,128)}) custom-call(f32[16,144,128]{2,1,0:T(8,128)S(1)} %get-tuple-element.15.carried, f32[128,128]{1,0:T(8,128)S(1)} %bitcast.24, f32[128,128]{1,0:T(8,128)S(1)} %bitcast.28, f32[128,128]{1,0:T(8,128)S(1)} %bitcast.29, s32[128,128]{1,0:T(8,128)S(1)} %bitcast.26, f32[128,128]{1,0:T(8,128)S(1)} %copy-done.8, ...), custom_call_target="tpu_custom_call" | custom-call | tf_op jit(solution)/shard_map/flux/pallas_call | solution.py:548
Async XLA Ops:
  0.6 20.2 %copy-start.9 = (s32[256]{0:T(256)S(1)}, s32[256]{0:T(256)}, u32[]{:S(2)}) copy-start(s32[256]{0:T(256)} %param.39) | copy-start | bytes 3076
  0.6 20.2 %copy-start.10 = (s32[256,1]{0,1:T(1,128)S(1)}, s32[256,1]{0,1:T(1,128)}, u32[]{:S(2)}) copy-start(s32[256,1]{0,1:T(1,128)} %param.40) | copy-start | bytes 3076
  0.7 20.2 %copy-start.11 = (s32[256]{0:T(256)S(1)}, s32[256]{0:T(256)}, u32[]{:S(2)}) copy-start(s32[256]{0:T(256)} %param.41) | copy-start | bytes 3076
  0.7 20.2 %copy-start.12 = (f32[256]{0:T(256)S(1)}, f32[256]{0:T(256)}, u32[]{:S(2)}) copy-start(f32[256]{0:T(256)} %param.42) | copy-start | bytes 3076
  0.7 20.2 %copy-start.13 = (s32[1,16]{1,0:T(1,128)S(1)}, s32[1,16]{1,0:T(1,128)}, u32[]{:S(2)}) copy-start(s32[1,16]{1,0:T(1,128)} %place.1) | copy-start | bytes 196
  0.7 20.2 %copy-start.14 = (f32[1,32]{1,0:T(1,128)S(1)}, f32[1,32]{1,0:T(1,128)}, u32[]{:S(2)}) copy-start(f32[1,32]{1,0:T(1,128)} %own_press.1) | copy-start | bytes 388
  0.7 20.2 %copy-start.15 = (s32[1,32]{1,0:T(1,128)S(1)}, s32[1,32]{1,0:T(1,128)}, u32[]{:S(2)}) copy-start(s32[1,32]{1,0:T(1,128)} %order.1) | copy-start | bytes 388
  5.2 0.7 %copy-start.4 = (f32[3,128,128]{2,1,0:T(8,128)}, f32[3,128,128]{2,1,0:T(8,128)S(1)}, u32[]{:S(2)}) copy-start(f32[3,128,128]{2,1,0:T(8,128)S(1)} %get-tuple-element.25.terms) | copy-start | bytes 589828
  5.9 0.6 %copy-start.7 = (f32[128,128]{1,0:T(8,128)}, f32[128,128]{1,0:T(8,128)S(1)}, u32[]{:S(2)}) copy-start(f32[128,128]{1,0:T(8,128)S(1)} %get-tuple-element.16.mob) | copy-start | bytes 196612
  6.5 14.4 %copy-start = (f32[16,8,16,128]{3,2,1,0:T(8,128)S(1)}, f32[16,8,16,128]{3,2,1,0:T(8,128)}, u32[]{:S(2)}) copy-start(f32[16,8,16,128]{3,2,1,0:T(8,128)} %param.30) | copy-start | bytes 3145732
  6.5 14.5 %copy-start.1 = (f32[8,16,128]{2,1,0:T(8,128)S(1)}, f32[8,16,128]{2,1,0:T(8,128)}, u32[]{:S(2)}) copy-start(f32[8,16,128]{2,1,0:T(8,128)} %param.25) | copy-start | bytes 196612
  6.5 14.4 %collective-permute-start.2 = (f32[18,16,128]{2,1,0:T(8,128)}, f32[18,16,128]{2,1,0:T(8,128)}, u32[]{:S(2)}, u32[]{:S(2)}) collective-permute-start(f32[18,16,128]{2,1,0:T(8,128)} %bitcast.16), channel_id=1, source_target_pairs={{0,16},{16,0},{1,17},{17,1},{2,18},{18,2},{3,19},{19,3},{4,20},{20... | collective-permute-start | bytes 442376 | tf_op jit(solution)/shard_map/ppermute | solution.py:531
  9.5 11.4 %collective-permute-start = (f32[18,8,128]{2,1,0:T(8,128)}, f32[18,8,128]{2,1,0:T(8,128)}, u32[]{:S(2)}, u32[]{:S(2)}) collective-permute-start(f32[18,8,128]{2,1,0:T(8,128)} %get-tuple-element.17), channel_id=1, source_target_pairs={{0,1},{2,3},{4,5},{6,7},{8,9},{10,11},{12,13},{14,15},{1,0},{3,2},... | collective-permute-start | bytes 221192 | tf_op jit(solution)/shard_map/ppermute | solution.py:533
  9.5 11.4 %collective-permute-start.1 = (f32[18,8,128]{2,1,0:T(8,128)}, f32[18,8,128]{2,1,0:T(8,128)}, u32[]{:S(2)}, u32[]{:S(2)}) collective-permute-start(f32[18,8,128]{2,1,0:T(8,128)} %get-tuple-element.18), channel_id=1, source_target_pairs={{0,16},{1,2},{2,1},{3,4},{4,3},{5,6},{6,5},{7,8},{8,7},{9,10},{10,... | collective-permute-start | bytes 221192 | tf_op jit(solution)/shard_map/ppermute | solution.py:532
  9.5 11.3 %all-to-all-start = ((f32[16,1,128]{2,1,0:T(1,128)}), f32[16,1,128]{2,1,0:T(1,128)S(1)}, u32[]{:S(2)}, u32[]{:S(2)}) async-start(f32[16,1,128]{2,1,0:T(1,128)} %bitcast.12), calls=%async_computation | async-start | bytes 16384 | tf_op jit(solution)/shard_map/all_to_all | solution.py:528
  19.0 0.9 %copy-start.5 = (f32[3,128,128]{2,1,0:T(8,128)S(1)}, f32[3,128,128]{2,1,0:T(8,128)}, u32[]{:S(2)}) copy-start(f32[3,128,128]{2,1,0:T(8,128)} %copy-done.4) | copy-start | bytes 589828
  21.0 0.8 %copy-start.2 = (s32[8,16,128]{2,1,0:T(8,128)S(1)}, s32[8,16,128]{2,1,0:T(8,128)}, u32[]{:S(2)}) copy-start(s32[8,16,128]{2,1,0:T(8,128)} %param.27) | copy-start | bytes 196612
  21.8 0.8 %copy-start.3 = (f32[8,16,128]{2,1,0:T(8,128)S(1)}, f32[8,16,128]{2,1,0:T(8,128)}, u32[]{:S(2)}) copy-start(f32[8,16,128]{2,1,0:T(8,128)} %param.28) | copy-start | bytes 196612
  22.7 0.8 %copy-start.6 = (f32[8,16,128]{2,1,0:T(8,128)S(1)}, f32[8,16,128]{2,1,0:T(8,128)}, u32[]{:S(2)}) copy-start(f32[8,16,128]{2,1,0:T(8,128)} %param.29) | copy-start | bytes 196612
  23.5 0.8 %copy-start.8 = (f32[128,128]{1,0:T(8,128)S(1)}, f32[128,128]{1,0:T(8,128)}, u32[]{:S(2)}) copy-start(f32[128,128]{1,0:T(8,128)} %copy-done.7) | copy-start | bytes 196612
where the time goes:
time: 28.3 us; the launch traced here: 27.9 us
  starting transfers between devices  11.2 us (40%)
  Pallas kernels  8.89 us (31%)
  local copies, waits for them, and re-layouts  5.6 us (20%)
  between operations  2.14 us (8%)
    all_to_all x1, starting transfers between devices, per_device(): lax.all_to_all(part, 'sub', split_axis=0, concat_axis=0, axis_index_group...  8.21 us
    unnamed x32, local copies, waits for them, and re-layouts  5.6 us
    pallas_call x1, Pallas kernels, per_device(): pl.pallas_call(functools.partial(phase_kernel, nx, ny, axes), out_shape=(...  4.49 us
    pallas_call x1, Pallas kernels, per_device(): pl.pallas_call(functools.partial(flux_kernel, nx, ny, axes, many_x), out_...  3.54 us
    ppermute x1, starting transfers between devices, per_device(): lax.ppermute(edge_x[k], 'grp', swaps_of(ng, k == 1))  2.94 us
    pallas_call x1, Pallas kernels, per_device(): pl.pallas_call(functools.partial(fugacity_kernel, ny), out_shape=jax.Shap...  0.86 us
  transfers between devices with their start and end apart: 4, of which 0 were waited for; matrix products, arithmetic and copies ran while one was open for 0% of the time, Pallas kernels for 3%

commit v1 on v0

--- a/solution.py
+++ b/solution.py
@@ -152,90 +152,93 @@
     (heat,) = arrived("heat")
 
     shape3 = (ny // SUBLANES, SUBLANES, LANES)
+    for load in loads:
+        load.wait()
+    root_t = [jnp.sqrt(heat[pl.ds(x * ny, ny)].reshape(shape3)) for x in range(nx)]
+    for x in range(nx):
+        span, lanes = pl.ds(x * ny, ny), pl.ds(x * LANES, LANES)
+        total = jnp.zeros(shape3, F32)
+        volume = jnp.zeros(shape3, F32)
+        for i in range(nc):
+            o = amount_v[i, span].reshape(shape3)
+            v = jnp.abs(table_v[0, i] - table_v[1, i] * root_t[x]) * o
+            total += o
+            volume += table_v[2, i] * o
+            high, low = pieces_of(v.reshape(ny, LANES), 2)
+            split_v[pl.ds(i * ny, ny), lanes] = high
+            split_v[pl.ds(size + i * ny, ny), lanes] = low
+            split_v[pl.ds(2 * size + i * ny, ny), lanes] = high
+        field_v[0, span] = total.reshape(ny, LANES)
+        field_v[1, span] = volume.reshape(ny, LANES)
+    for c in range(chunks):
+        mixed = mat(mixer, split_v[:, pl.ds(c * per * LANES, per * LANES)])
+        for k in range(per):
+            x = c * per + k
+            span = pl.ds(x * ny, ny)
+            total = jnp.zeros(shape3, F32)
+            for i in range(nc):
+                m = mixed[i * ny : (i + 1) * ny, k * LANES : (k + 1) * LANES].reshape(shape3)
+                psi = jnp.abs(table_v[0, i] - table_v[1, i] * root_t[x]) * m
+                total += amount_v[i, span].reshape(shape3) * psi
+                psi_v[i, span] = psi.reshape(ny, LANES)
+            field_v[2, span] = total.reshape(ny, LANES)
+
+    flag, visc, trans, inject = arrived("flag", "visc", "trans", "inject")
+    states = []
     for h in range(2):
-        loads[h].wait()
-        for c in range(h * half, (h + 1) * half):
-            for x in range(c * per, (c + 1) * per):
-                span = pl.ds(x * ny, ny)
-                lanes = pl.ds(x * LANES, LANES)
-                root_t = jnp.sqrt(heat[span].reshape(shape3))
-                total = jnp.zeros(shape3, F32)
-                volume = jnp.zeros(shape3, F32)
-                for i in range(nc):
-                    o = amount_v[i, span].reshape(shape3)
-                    v = jnp.abs(table_v[0, i] - table_v[1, i] * root_t) * o
-                    total += o
-                    volume += table_v[2, i] * o
-                    high, low = pieces_of(v.reshape(ny, LANES), 2)
-                    split_v[pl.ds(i * ny, ny), lanes] = high
-                    split_v[pl.ds(size + i * ny, ny), lanes] = low
-                    split_v[pl.ds(2 * size + i * ny, ny), lanes] = high
-                field_v[0, span] = total.reshape(ny, LANES)
-                field_v[1, span] = volume.reshape(ny, LANES)
-            lanes = pl.ds(c * per * LANES, per * LANES)
-            mixed = mat(mixer, split_v[:, lanes])
-            for k in range(per):
-                x = c * per + k
-                span = pl.ds(x * ny, ny)
-                root_t = jnp.sqrt(heat[span].reshape(shape3))
-                total = jnp.zeros(shape3, F32)
-                for i in range(nc):
-                    m = mixed[i * ny : (i + 1) * ny, k * LANES : (k + 1) * LANES].reshape(shape3)
-                    psi = jnp.abs(table_v[0, i] - table_v[1, i] * root_t) * m
-                    total += amount_v[i, span].reshape(shape3) * psi
-                    psi_v[i, span] = psi.reshape(ny, LANES)
-                field_v[2, span] = total.reshape(ny, LANES)
-
-        if h == 0:
-            flag, visc, trans, inject = arrived("flag", "visc", "trans", "inject")
         span = pl.ds(h * half * rows, half * rows)
         p, t = press[span], heat[span]
         liquid = flag[span] == 1
         r = inverse(field_v[0, span])
         rt = inverse(t)
         ratio_pt = p * rt
-        g = ratio_pt * rt
         beta = field_v[1, span] * r
-        gr = g * r
+        gr = ratio_pt * rt * r
         big_a = gr * r * field_v[2, span]
         big_b = ratio_pt * beta
         z = jnp.where(liquid, big_b + 0.01, 1.0 + big_b)
-        floor = big_b + 0.01
-        c2 = big_b - 1.0
         c1 = big_a - 3.0 * big_b * big_b - 2.0 * big_b
         c0 = big_b * big_b + big_b * big_b * big_b - big_a * big_b
-        twice = 2.0 * c2
-        for _ in range(NEWT):
-            value = ((z + c2) * z + c1) * z + c0
-            incline = (3.0 * z + twice) * z + c1
-            z = jnp.maximum(z - value * inverse(jnp.maximum(incline, 0.1)), floor)
+        states.append([z, big_b, big_b + 0.01, big_b - 1.0, c1, c0])
+        field_v[1, span] = inverse(beta)
+        field_v[3, span] = r
+        terms_out[0, span] = ratio_pt
+        terms_out[1, span] = 0.5 * big_a
+        terms_out[2, span] = gr
+    for _ in range(NEWT):
+        for state in states:
+            z, _, floor, c2, c1, c0 = state
+            near = z + c2
+            value = (near * z + c1) * z + c0
+            incline = (near + near + z) * z + c1
+            state[0] = jnp.maximum(z - value * inverse(jnp.maximum(incline, 0.1)), floor)
+    for h, (z, big_b, *_) in enumerate(states):
+        span = pl.ds(h * half * rows, half * rows)
+        ratio_pt, gr = terms_out[0, span], terms_out[2, span]
         log_ratio = jnp.log(
             (z + (1.0 + ROOT_TWO) * big_b) * inverse(z + (1.0 - ROOT_TWO) * big_b)
         )
         lb = log_ratio * inverse(ROOT_TWO * big_b)
-        e0 = jnp.log(z - big_b)
-        e1 = (z - 1.0 + 0.5 * big_a * lb) * inverse(beta)
-        e2 = gr * lb
-        mob = ratio_pt * inverse(z * jnp.where(liquid, visc[1], visc[0]))
+        mob = ratio_pt * inverse(z * jnp.where(flag[span] == 1, visc[1], visc[0]))
         mob_out[span] = mob
-        terms_out[0, span] = e0
-        terms_out[1, span] = e1
-        terms_out[2, span] = e2
-        field_v[3, span] = mob * r
-        for x in range(h * half * per, (h + 1) * half * per):
-            span = pl.ds(x * ny, ny)
-            mr = field_v[3, span]
-            for i in range(nc):
-                carried_out[i, pl.ds(MARGIN + x * ny, ny)] = mr * amount_v[i, span]
+        field_v[3, span] = mob * field_v[3, span]
+        terms_out[0, span] = jnp.log(z - big_b)
+        terms_out[1, span] = (z - 1.0 + terms_out[1, span] * lb) * field_v[1, span]
+        terms_out[2, span] = gr * lb
+    for x in range(nx):
+        span = pl.ds(x * ny, ny)
+        mr = field_v[3, span]
+        for i in range(nc):
+            carried_out[i, pl.ds(MARGIN + x * ny, ny)] = mr * amount_v[i, span]
 
     total = sum(inject[i] for i in range(nc))
-    share = 1.0 / jnp.full((SUBLANES, LANES), total, F32)
+    share = 1.0 / jnp.full((1, LANES), total, F32)
     numbers = [trans[0], trans[1], trans[2], visc[0], visc[1]]
     for i in range(nc):
-        consts_out[i] = inject[i] * share
-        consts_out[nc + 8 + i] = table_v[2, i]
+        consts_out[pl.ds(i, 1)] = inject[i] * share
+        consts_out[pl.ds(nc + 8 + i, 1)] = jnp.full((1, LANES), covol[i], F32)
     for i, number in enumerate(numbers):
-        consts_out[nc + i] = jnp.full((SUBLANES, LANES), number, F32)
+        consts_out[pl.ds(nc + i, 1)] = jnp.full((1, LANES), number, F32)
 
     seg, strength, own_press, perm = arrived("seg", "strength", "own_press", "perm")
     weight = strength[...] * cells_of(mob_out[...], 2)
@@ -266,16 +269,15 @@
 
 def fugacity_kernel(ny, psi, terms, consts, lnphi_out, lnphi_v, sems):
     nc, rows, _ = psi.shape
-    shape3 = (ny // SUBLANES, SUBLANES, LANES)
     parts = sems.shape[0]
     stores = []
     for part in range(parts):
         for x in range(part * rows // parts // ny, (part + 1) * rows // parts // ny):
             span = pl.ds(x * ny, ny)
-            e0, e1, e2 = (terms[k, span].reshape(shape3) for k in range(3))
+            e0, e1, e2 = (terms[k, span] for k in range(3))
             for i in range(nc):
-                value = consts[nc + 8 + i] * e1 - e0 - psi[i, span].reshape(shape3) * e2
-                lnphi_v[i, span] = value.reshape(ny, LANES).astype(BF16)
+                value = consts[pl.ds(nc + 8 + i, 1)] * e1 - e0 - psi[i, span] * e2
+                lnphi_v[i, span] = value.astype(BF16)
         span = pl.ds(part * rows // parts, rows // parts)
         copy = pltpu.make_async_copy(lnphi_v.at[:, span], lnphi_out.at[:, span], sems.at[part])
         copy.start()
@@ -290,12 +292,12 @@
     axes,
     many_x,
     carried,
-    press,
-    perm,
-    pore,
-    flag,
+    press_in,
+    perm_in,
+    pore_in,
+    flag_in,
+    old_in,
     mob,
-    old,
     edge_ya,
     edge_yb,
     well_rows,
@@ -312,8 +314,16 @@
     friction,
     *rest,
 ):
-    edge_x, (resid_out, well_out, y_v, res_v, out_sems) = rest[:many_x], rest[many_x:]
+    edge_x, rest = rest[:many_x], rest[many_x:]
+    resid_out, well_out, press, perm, pore, flag, old, y_v, res_v, in_sems, out_sems = rest
     nc = carried.shape[0]
+    loads = []
+    for k, (source, target) in enumerate(
+        ((press_in, press), (perm_in, perm), (pore_in, pore), (flag_in, flag), (old_in, old))
+    ):
+        copy = pltpu.make_async_copy(source, target, in_sems.at[k])
+        copy.start()
+        loads.append(copy)
     g, s = lax.axis_index(axes[0]), lax.axis_index(axes[1])
     ng, ns = lax.axis_size(axes[0]), lax.axis_size(axes[1])
     odd_g, odd_s = g % 2 == 1, s % 2 == 1
@@ -368,9 +378,11 @@
     first, final = row == 0, row == ny - 1
 
     def const(k):
-        return jnp.concatenate([consts[k]] * (ny // SUBLANES), axis=0)
+        return jnp.broadcast_to(consts[pl.ds(k, 1)], (ny, LANES))
 
     stores = []
+    for load in loads:
+        load.wait()
     for x in range(nx):
         rows = pl.ds(x * ny, ny)
         p_a, k_a = press[rows], perm[rows]
@@ -507,7 +519,7 @@
             jax.ShapeDtypeStruct((nc + 2, nx, nz), F32),
             jax.ShapeDtypeStruct((wells, LANES), F32),
             jax.ShapeDtypeStruct((1, perfs), F32),
-            jax.ShapeDtypeStruct((2 * nc + 8, SUBLANES, LANES), F32),
+            jax.ShapeDtypeStruct((2 * nc + 8, LANES), F32),
         ),
         in_specs=[hbm] * (1 + len(sources)),
         out_specs=(vm,) * 10,
@@ -551,17 +563,19 @@
             jax.ShapeDtypeStruct((nc, rows, nz), F32),
             jax.ShapeDtypeStruct((1, segments), F32),
         ),
-        in_specs=[vm] * (21 + many_x),
+        in_specs=[vm] + [hbm] * 5 + [vm] * (15 + many_x),
         out_specs=(hbm, vm),
         scratch_shapes=[
+            *(pltpu.VMEM(a.shape, a.dtype) for a in (press, perm, pore, flag, old)),
             pltpu.VMEM((2, nc + 2, nx, nz), F32),
             pltpu.VMEM((nc, rows, nz), F32),
+            pltpu.SemaphoreType.DMA((5,)),
             pltpu.SemaphoreType.DMA((nx,)),
         ],
         compiler_params=pltpu.CompilerParams(vmem_limit_bytes=VMEM_LIMIT),
         name="flux",
     )(
-        carried, press, perm, pore, flag, mob, old, got_ya, got_yb, well_rows,
+        carried, *(in_hbm(a) for a in (press, perm, pore, flag, old)), mob, got_ya, got_yb, well_rows,
         locale, member, seg, strength, place, pcell,
         consts, seg_press, order, exit_press, friction, *got_x,
     )

time: 28.3 us -> 22.4 us (0.79)
  local copies, waits for them, and re-layouts: 5.6 us -> 0.04 us
    unnamed x32 -> x14, local copies, waits for them, and re-layouts: 5.6 us -> 0.04 us
  transfers between devices with their start and end apart: 4 -> 4, of which waited for: 0 -> 0; matrix products, arithmetic and copies ran while one was open for 0% -> 0% of each run, Pallas kernels for 3% -> 4%
where the time goes in v1:
time: 22.4 us; the launch traced here: 22.2 us
  starting transfers between devices  11.3 us (50%)
  Pallas kernels  8.72 us (39%)
  between operations  2.07 us (9%)
    all_to_all x1, starting transfers between devices, per_device(): lax.all_to_all(part, 'sub', split_axis=0, concat_axis=0, axis_index_group...  8.15 us
    pallas_call x1, Pallas kernels, per_device(): pl.pallas_call(functools.partial(phase_kernel, nx, ny, axes), out_shape=(...  4.25 us
    pallas_call x1, Pallas kernels, per_device(): pl.pallas_call(functools.partial(flux_kernel, nx, ny, axes, many_x), out_...  3.61 us
    ppermute x1, starting transfers between devices, per_device(): lax.ppermute(edge_x[k], 'grp', swaps_of(ng, k == 1))  3 us
    pallas_call x1, Pallas kernels, per_device(): pl.pallas_call(functools.partial(fugacity_kernel, ny), out_shape=jax.Shap...  0.86 us
  transfers between devices with their start and end apart: 4, of which 0 were waited for; matrix products, arithmetic and copies ran while one was open for 0% of the time, Pallas kernels for 4%

profile of v1, /device:TPU:0, one launch (start us, length us, event | category | flops | bytes accessed | tf_op | source)
XLA Modules:
  0.0 22.2 jit_solution(11813646886595647864)
XLA Ops:
  0.6 4.2 %phase.1 = (f32[16,128,128]{2,1,0:T(8,128)S(1)}, f32[3,128,128]{2,1,0:T(8,128)S(1)}, f32[16,144,128]{2,1,0:T(8,128)S(1)}, f32[128,128]{1,0:T(8,128)S(1)}, f32[1,...) custom-call(f32[16,128,128]{2,1,0:T(8,128)} %bitcast.33, ...), custom_call_target="tpu_custom_call" | custom-call | tf_op jit(solution)/shard_map/phase/pallas_call | solution.py:510
  4.9 0.0 copy-start
  4.9 0.0 copy-start.1
  4.9 0.0 copy-start.2
  4.9 0.0 copy-start.3
  4.9 0.0 copy-start.4
  4.9 0.0 copy-start.5
  5.0 0.0 copy-start.6
  5.0 3.0 %collective-permute-start.2 = (f32[18,16,128]{2,1,0:T(8,128)S(1)}, f32[18,16,128]{2,1,0:T(8,128)S(1)}, u32[]{:S(2)}, u32[]{:S(2)}) collective-permute-start(f32[18,16,128]{2,1,0:T(8,128)S(1)} %bitcast.31), channel_id=1, source_target_pairs={{0,16},{16,0},{1,17},{17,1},{2,18},{18,2},{3,19},{19,3},{4,20},{20... | collective-permute-start | bytes 442376 | tf_op jit(solution)/shard_map/ppermute | solution.py:543
  8.0 0.0 collective-permute-start
  8.0 0.2 collective-permute-start.1
  8.1 8.2 %all-to-all-start = ((f32[16,1,128]{2,1,0:T(1,128)}), f32[16,1,128]{2,1,0:T(1,128)S(1)}, u32[]{:S(2)}, u32[]{:S(2)}) async-start(f32[16,1,128]{2,1,0:T(1,128)} %bitcast.12), calls=%async_computation | async-start | bytes 16384 | tf_op jit(solution)/shard_map/all_to_all | solution.py:540
  17.6 0.9 %fugacity.1 = bf16[16,128,128]{2,1,0:T(8,128)(2,1)} custom-call(f32[16,128,128]{2,1,0:T(8,128)S(1)} %get-tuple-element.24.psi, f32[3,128,128]{2,1,0:T(8,128)S(1)} %get-tuple-element.25.terms, f32[40,128]{1,0:T(8,128)S(1)} %get-tuple-element.21.consts), custom_call_target="tpu_custom_call" | custom-call | flops 2097152 | bytes 8388608 | tf_op jit(solution)/shard_map/fugacity/pallas_call | solution.py:547
  18.5 0.0 all-to-all-done
  18.5 0.0 collective-permute-done.edge_ya
  18.5 0.0 collective-permute-done.1.edge_yb
  18.5 0.0 collective-permute-done.2.rest_0_
  18.5 0.0 copy-done
  18.5 0.0 copy-done.1
  18.5 0.0 copy-done.2
  18.5 0.0 copy-done.3
  18.5 0.0 copy-done.4
  18.6 0.0 copy-done.5
  18.6 0.0 copy-done.6
  18.6 3.6 %flux.1 = (f32[16,128,128]{2,1,0:T(8,128)}, f32[1,32]{1,0:T(1,128)}) custom-call(f32[16,144,128]{2,1,0:T(8,128)S(1)} %get-tuple-element.15.carried, f32[128,128]{1,0:T(8,128)} %bitcast.36, f32[128,128]{1,0:T(8,128)} %bitcast.40, f32[128,128]{1,0:T(8,128)} %bitcast.42, s32[128,128]{1,0:T(8,128)} %bitcast.38, f32[16,128,128]{2,1,0:T(8,128)} %bitcast.32, ...), custom_call_target="tpu_custom_call" | custom-call | tf_op jit(solution)/shard_map/flux/pallas_call | solution.py:560
Async XLA Ops:
  4.9 13.6 %copy-start = (s32[256]{0:T(256)S(1)}, s32[256]{0:T(256)}, u32[]{:S(2)}) copy-start(s32[256]{0:T(256)} %param.39) | copy-start | bytes 3076
  4.9 13.6 %copy-start.1 = (s32[256,1]{0,1:T(1,128)S(1)}, s32[256,1]{0,1:T(1,128)}, u32[]{:S(2)}) copy-start(s32[256,1]{0,1:T(1,128)} %param.40) | copy-start | bytes 3076
  4.9 13.6 %copy-start.2 = (s32[256]{0:T(256)S(1)}, s32[256]{0:T(256)}, u32[]{:S(2)}) copy-start(s32[256]{0:T(256)} %param.41) | copy-start | bytes 3076
  4.9 13.6 %copy-start.3 = (f32[256]{0:T(256)S(1)}, f32[256]{0:T(256)}, u32[]{:S(2)}) copy-start(f32[256]{0:T(256)} %param.42) | copy-start | bytes 3076
  4.9 13.6 %copy-start.4 = (s32[1,16]{1,0:T(1,128)S(1)}, s32[1,16]{1,0:T(1,128)}, u32[]{:S(2)}) copy-start(s32[1,16]{1,0:T(1,128)} %place.1) | copy-start | bytes 196
  4.9 13.6 %copy-start.5 = (f32[1,32]{1,0:T(1,128)S(1)}, f32[1,32]{1,0:T(1,128)}, u32[]{:S(2)}) copy-start(f32[1,32]{1,0:T(1,128)} %own_press.1) | copy-start | bytes 388
  5.0 13.6 %copy-start.6 = (s32[1,32]{1,0:T(1,128)S(1)}, s32[1,32]{1,0:T(1,128)}, u32[]{:S(2)}) copy-start(s32[1,32]{1,0:T(1,128)} %order.1) | copy-start | bytes 388
  5.0 13.5 %collective-permute-start.2 = (f32[18,16,128]{2,1,0:T(8,128)S(1)}, f32[18,16,128]{2,1,0:T(8,128)S(1)}, u32[]{:S(2)}, u32[]{:S(2)}) collective-permute-start(f32[18,16,128]{2,1,0:T(8,128)S(1)} %bitcast.31), channel_id=1, source_target_pairs={{0,16},{16,0},{1,17},{17,1},{2,18},{18,2},{3,19},{19,3},{4,20},{20... | collective-permute-start | bytes 442376 | tf_op jit(solution)/shard_map/ppermute | solution.py:543
  8.0 10.5 %collective-permute-start = (f32[18,8,128]{2,1,0:T(8,128)S(1)}, f32[18,8,128]{2,1,0:T(8,128)S(1)}, u32[]{:S(2)}, u32[]{:S(2)}) collective-permute-start(f32[18,8,128]{2,1,0:T(8,128)S(1)} %get-tuple-element.17), channel_id=1, source_target_pairs={{0,1},{2,3},{4,5},{6,7},{8,9},{10,11},{12,13},{14,15},{1,0},{3,2},... | collective-permute-start | bytes 221192 | tf_op jit(solution)/shard_map/ppermute | solution.py:545
  8.0 10.5 %collective-permute-start.1 = (f32[18,8,128]{2,1,0:T(8,128)S(1)}, f32[18,8,128]{2,1,0:T(8,128)S(1)}, u32[]{:S(2)}, u32[]{:S(2)}) collective-permute-start(f32[18,8,128]{2,1,0:T(8,128)S(1)} %get-tuple-element.18), channel_id=1, source_target_pairs={{0,16},{1,2},{2,1},{3,4},{4,3},{5,6},{6,5},{7,8},{8,7},{9,10},{10,... | collective-permute-start | bytes 221192 | tf_op jit(solution)/shard_map/ppermute | solution.py:544
  8.1 10.4 %all-to-all-start = ((f32[16,1,128]{2,1,0:T(1,128)}), f32[16,1,128]{2,1,0:T(1,128)S(1)}, u32[]{:S(2)}, u32[]{:S(2)}) async-start(f32[16,1,128]{2,1,0:T(1,128)} %bitcast.12), calls=%async_computation | async-start | bytes 16384 | tf_op jit(solution)/shard_map/all_to_all | solution.py:540
